TPU v7x, 512 devices: a whole 4x8x8 slice. The times are simulated.
512 devices in a mesh: row: 32 (over x, y_hi, core), col: 16 (over z, y_lo).
Axes of the slice: x: 4, y: 8 (y_hi: 4, y_lo: 2; y = y_hi * 2 + y_lo), z: 8, core: 2. Of those that a mesh axis runs over, the one named last changes fastest.
Arguments:
- tokens: bfloat16 [8192, 3072], P('row', 'col'), may hold values from -6 to 6
- w_in: bfloat16 [3072, 12288], P('row', 'col'), may hold values from -0.109375 to 0.109375
- w_out: bfloat16 [12288, 3072], P('row', 'col'), may hold values from -0.0546875 to 0.0546875
Outputs:
- mixed: bfloat16 [8192, 3072], P('row', 'col')
All inputs are finite; a program needn't handle non-finite values.
Results may differ from a plain program's by a relative error of at most 0.0049.
Values may be sent and summed in bfloat16 or wider, within the bound.
A program may use at most 64 MiB of HBM per device.

v0:
```python
import jax
import jax.numpy as jnp
from jax import lax
from jax.sharding import PartitionSpec as P


def local(tokens, w_in, w_out):
    token_rows = lax.all_gather(tokens, "col", axis=1, tiled=True)
    columns = token_rows
    pre = jnp.dot(
        columns, lax.all_gather(w_in, "row", axis=0, tiled=True), preferred_element_type=jnp.float32
    )
    hidden = jax.nn.gelu(pre, approximate=False).astype(jnp.bfloat16)
    hidden_rows = lax.all_gather(hidden, "col", axis=1, tiled=True)
    columns = hidden_rows
    mixed = jnp.dot(
        columns,
        lax.all_gather(w_out, "row", axis=0, tiled=True),
        preferred_element_type=jnp.float32,
    )
    return mixed.astype(jnp.bfloat16)


def solution(mesh):
    placed = (P("row", "col"), P("row", "col"), P("row", "col"))
    return jax.shard_map(
        local, mesh=mesh, in_specs=placed, out_specs=P("row", "col"), check_vma=False
    )
```

profile of v0, /device:TPU:1, one launch (start us, length us, event | category | flops | bytes accessed | tf_op | source)
XLA Modules:
  0.0 393.3 jit_solution(3836444676025672992)
XLA Ops:
  6.5 0.0 all-gather.5.cloned.1.call-start
  6.5 0.7 all-gather.5.cloned.1.call-update
  7.3 0.0 all-gather.7.cloned.1.call-start
  7.3 0.7 all-gather.7.cloned.1.call-update
  8.0 0.0 all-gather.11.cloned.1.call-start
  8.1 0.7 all-gather.11.cloned.1.call-update
  8.7 0.0 all-gather.9.cloned.1.call-start
  8.8 72.8 %all-gather.5.cloned.1.call-done = bf16[256,3072]{0,1:T(8,128)(2,1)} async-done(((bf16[256,192]{0,1:T(8,128)(2,1)}), bf16[256,3072]{0,1:T(8,128)(2,1)}) %all-gather.5.cloned.1.call-update) | async-done | bytes 1572880 | tf_op jit(solution)/shard_map/all_gather | solution.py:8
  81.6 80.2 %all-gather.7.cloned.1.call-done = bf16[3072,768]{1,0:T(8,128)(2,1)} async-done(((bf16[96,768]{1,0:T(8,128)(2,1)}), bf16[3072,768]{1,0:T(8,128)(2,1)}) %all-gather.7.cloned.1.call-update) | async-done | bytes 4718608 | tf_op jit(solution)/shard_map/all_gather | solution.py:11
  161.9 6.5 %fusion.2 = bf16[256,768]{1,0:T(8,128)(2,1)} fusion(bf16[256,3072]{0,1:T(8,128)(2,1)} %all-gather.5.cloned.1.call-done, bf16[3072,768]{1,0:T(8,128)(2,1)} %all-gather.7.cloned.1.call-done), kind=kOutput, calls=%fused_computation.4 | convolution fusion | flops 1220739072 | bytes 6684672 | tf_op jit(solution)/shard_map/dot_general | solution.py:10
  168.4 0.0 all-gather.9.cloned.1.call-update
  168.4 66.5 %all-gather.11.cloned.1.call-done = bf16[12288,192]{0,1:T(8,128)(2,1)} async-done(((bf16[384,192]{0,1:T(8,128)(2,1)}), bf16[12288,192]{0,1:T(8,128)(2,1)}) %all-gather.11.cloned.1.call-update) | async-done | bytes 4718608 | tf_op jit(solution)/shard_map/all_gather | solution.py:18
  234.9 144.8 %all-gather.9.cloned.1.call-done = bf16[256,12288]{1,0:T(8,128)(2,1)} async-done(((bf16[256,768]{1,0:T(8,128)(2,1)}), bf16[256,12288]{1,0:T(8,128)(2,1)}) %all-gather.9.cloned.1.call-update) | async-done | bytes 6291472 | tf_op jit(solution)/shard_map/all_gather | solution.py:14
  379.7 7.0 %convolution_convert_fusion = bf16[256,192]{0,1:T(8,128)(2,1)} fusion(bf16[256,12288]{1,0:T(8,128)(2,1)} %all-gather.9.cloned.1.call-done, bf16[12288,192]{0,1:T(8,128)(2,1)} %all-gather.11.cloned.1.call-done), kind=kOutput, calls=%fused_computation.1 | convolution fusion | flops 1208008704 | bytes 11108352 | tf_op jit(solution)/shard_map/dot_general | solution.py:16
Async XLA Ops:
  6.5 75.1 %all-gather.5.cloned.1.call-start = ((), (), s32[]{:S(2)}) async-start(), calls=%async_computation | async-start | bytes 1671168 | tf_op jit(solution)/shard_map/all_gather | solution.py:8
  7.3 154.6 %all-gather.7.cloned.1.call-start = ((), (), s32[]{:S(2)}) async-start(), calls=%async_computation.1 | async-start | bytes 4866048 | tf_op jit(solution)/shard_map/all_gather | solution.py:11
  8.0 226.9 %all-gather.11.cloned.1.call-start = ((), (), s32[]{:S(2)}) async-start(), calls=%async_computation.3 | async-start | bytes 4866048 | tf_op jit(solution)/shard_map/all_gather | solution.py:18
  8.7 371.0 %all-gather.9.cloned.1.call-start = ((), (), s32[]{:S(2)}) async-start(), calls=%async_computation.2 | async-start | bytes 6684672 | tf_op jit(solution)/shard_map/all_gather | solution.py:14
Sparse Core Ops, SparseCore 0:
  9.4 72.1 all-gather.4
  84.7 77.0 all-gather.6
  164.9 69.9 all-gather.10
  236.9 142.7 all-gather.8
where the time goes:
time: 393 us
  waiting for transfers between devices  366 us (93%)
  matrix products  13.5 us (3%)
  between operations  13.1 us (3%)
    all_gather x1, waiting for transfers between devices, local(): hidden_rows = lax.all_gather(hidden, 'col', axis=1, tiled=True)  145 us
    all_gather x1, waiting for transfers between devices, local(): lax.all_gather(w_in, 'row', axis=0, tiled=True)  80.2 us
    all_gather x1, waiting for transfers between devices, local(): token_rows = lax.all_gather(tokens, 'col', axis=1, tiled=True)  72.8 us
    all_gather x1, waiting for transfers between devices, local(): lax.all_gather(w_out, 'row', axis=0, tiled=True)  66.5 us
  transfers between devices with their start and end apart: 4, of which 4 were waited for; matrix products, arithmetic and copies ran while one was open for 2% of the time, Pallas kernels for 0%

commit v1 on v0

v1 whole, which is shorter than its diff:
```python
import jax
import jax.numpy as jnp
from jax import lax
from jax.experimental import pallas as pl
from jax.experimental.pallas import tpu as pltpu
from jax.sharding import PartitionSpec as P

MESH = pl.DeviceIdType.MESH
BF16, F32 = jnp.bfloat16, jnp.float32
SEMS = 128


def horner(v, terms):
    total = jnp.full_like(v, terms[0])
    for term in terms[1:]:
        total = total * v + term
    return total


ERF_NEAR = (7.853861353153693e-5, -8.010193625184903e-4, 5.188327685732524e-3, -2.685381193529856e-2,
            1.128358514861418e-1, -3.761262582423300e-1, 1.128379165726710e0)
ERFC_MID = (2.326819970068386e-2, -1.387039388740657e-1, 3.687424674597105e-1, -5.824733027278666e-1,
            6.210004621745983e-1, -4.944515323274145e-1, 3.404879937665872e-1, -2.741127028184656e-1,
            5.638259427386472e-1)
ERFC_FAR = (-1.047766399936249e1, 1.297719955372516e1, -7.495518717768503e0, 2.921019019210786e0,
            -1.015265279202700e0, 4.218463358204948e-1, -2.820767439740514e-1, 5.641895067754075e-1)


def gelu(v):
    u = v * (-(0.5**0.5))
    square = u * u
    size = jnp.maximum(jnp.abs(u), 0.5)
    near = 1.0 - u * horner(jnp.minimum(square, 1.0), ERF_NEAR)
    inverse = 1.0 / size
    y = inverse * inverse
    series = jnp.where(size < 2.0, horner(jnp.minimum(y, 1.0), ERFC_MID), horner(jnp.minimum(y, 0.25), ERFC_FAR))
    tail = jnp.exp(-square) * inverse * series
    far = jnp.where(u < 0.0, 2.0 - tail, tail)
    return 0.5 * v * jnp.where(jnp.abs(u) < 1.0, near, far)


def kernel(tok_ref, win_ref, wout_ref, out_ref, tk, wi, wo, tokp, woh, wop, hid, acc, part, rs_out, rs_in, end_out, end_in,
           send_sem, recv_sem, local_sem):
    r, c = lax.axis_index("row"), lax.axis_index("col")
    x, yh, p, z, yl = r // 8, (r // 2) % 4, r % 2, c // 2, c % 2

    def device(x, yh, p, z, yl):
        return ((x % 4) * 8 + (yh % 4) * 2 + p, (z % 8) * 2 + yl)

    right, left = device(x + 1, yh, p, z, yl), device(x + 3, yh, p, z, yl)
    far_y, near_y = device(x, yh + 1, p, z, yl), device(x, yh + 3, p, z, yl)
    up, down = device(x, yh, p, z + 1, yl), device(x, yh, p, z + 7, yl)
    pair, sibling = device(x, yh, p, z, 1 - yl), device(x, yh, 1 - p, z, yl)

    flip = (yh // 2 + z) % 2
    other_x = (z // 2 + 4 - x) % 4
    spread = [device(other_x, 2 * flip + half, p, z, yh % 2) for half in range(2)]
    spread_from = [device(other_x, 2 * flip + yl, p, z, half) for half in range(2)]
    lift = device(x, yh, p, 2 * other_x + flip, yl)
    lift_from = device(x, yh, p, 2 * ((z // 2 + x) % 4) + flip, yl)

    sems = [0]
    started = []

    def copy(src, dst, to, mark=None):
        k = sems[0]
        sems[0] += 1
        mark = k if mark is None else mark
        return pltpu.make_async_remote_copy(
            src_ref=src, dst_ref=dst, send_sem=send_sem.at[k], recv_sem=recv_sem.at[mark], device_id=to, device_id_type=MESH
        )

    def send(src, dst, to):
        made = copy(src, dst, to)
        made.start()
        started.append(made)
        return made

    def send_maybe(src, dst, to, mark=None):
        mark = sems[0] if mark is None else mark
        made = copy(src, dst, to, mark)
        here = jnp.logical_and(to[0] == r, to[1] == c)

        @pl.when(here)
        def _():
            pltpu.make_async_copy(src, dst, recv_sem.at[mark]).start()

        @pl.when(jnp.logical_not(here))
        def _():
            made.start()

        def end():
            @pl.when(jnp.logical_not(here))
            def _():
                made.wait_send()

        return made, end

    def w1(dx, dy, core, half=None):
        px, py = (x + dx) % 4, (yh + dy) % 4
        at = wi.at[2 * px + py // 2, py % 2, core]
        return at if half is None else at.at[pl.ds(48 * half, 48)]

    def w1_group(dx, core):
        return wi.at[pl.ds(2 * ((x + dx) % 4), 2), :, core]

    def w2(dx, dy, core, half=None):
        px, py = (x + dx) % 4, (yh + dy) % 4
        at = wo.at[2 * ((z // 2 + px) % 4) + (z + py // 2) % 2, core, py % 2]
        return at if half is None else at.at[pl.ds(96 * half, 96)]

    def w2_group(dx, core):
        return wo.at[pl.ds(2 * ((z // 2 + x + dx) % 4), 2), core]

    barrier = pltpu.get_barrier_semaphore()
    greeted = [right, left, far_y, near_y, up, down, pair, sibling, *spread_from, lift_from]
    for to in greeted:
        pl.semaphore_signal(barrier, inc=1, device_id=to, device_id_type=MESH)
    pl.semaphore_wait(barrier, len(greeted))

    own_w1 = pltpu.make_async_copy(win_ref, w1(0, 0, p), local_sem.at[0])
    own_tok = pltpu.make_async_copy(tok_ref, tokp.at[yl], local_sem.at[1])
    own_w1.start()
    own_tok.start()
    tok_pair = send(tok_ref, tokp.at[yl], pair)
    y1 = {d: send(win_ref, w1(0, 0, p), to) for d, to in ((-1, far_y), (1, near_y))}
    halves = [
        send_maybe(wout_ref.at[pl.ds(192 * half, 192)], woh.at[yl], spread[half], SEMS + yl) for half in range(2)
    ]

    class Gather:
        def __init__(self, at, group):
            self.at, self.group = at, group
            self.x, self.xh, self.yh, self.sib = {}, {}, {}, {}

        def y_own(self, src):
            self.y = {d: send(src, self.at(0, 0, p), to) for d, to in ((-1, far_y), (1, near_y))}

        def y_forward(self):
            self.y[-1].wait_recv()
            self.yh[0] = send(self.at(0, -1, p, 0), self.at(0, -1, p, 0), far_y)
            self.x_send(-1)
            self.y[1].wait_recv()
            self.yh[1] = send(self.at(0, 1, p, 1), self.at(0, 1, p, 1), near_y)
            self.x_send(1)

        def y_last(self):
            self.yh[0].wait_recv()
            self.yh[1].wait_recv()
            self.x_send(2)

        def x_send(self, dy, src=None):
            src = self.at(0, dy, p) if src is None else src
            for d, to in ((-1, right), (1, left)):
                self.x[d, dy] = send(src, self.at(0, dy, p), to)

        def x_forward(self, dy):
            self.x[-1, dy].wait_recv()
            self.xh[0, dy] = send(self.at(-1, dy, p, 0), self.at(-1, dy, p, 0), right)
            self.x[1, dy].wait_recv()
            self.xh[1, dy] = send(self.at(1, dy, p, 1), self.at(1, dy, p, 1), left)

        def x_last(self):
            for made in self.xh.values():
                made.wait_recv()

        def share(self, dx):
            self.sib[dx] = send(self.group(dx, p), self.group(dx, p), sibling)

    first, second = Gather(w1, w1_group), Gather(w2, w2_group)
    first.y = y1
    first.x_send(0, win_ref)

    tok_pair.wait_recv()
    own_tok.wait()
    tk[z] = jnp.concatenate([tokp[0], tokp[1]], axis=1)
    ring = {}
    ring[0, 0] = send(tk.at[z], tk.at[z], up)
    ring[1, 0] = send(tk.at[z], tk.at[z], down)

    for half in range(2):
        pltpu.make_async_copy(woh.at[half], woh.at[half], recv_sem.at[SEMS + half]).wait()
    wop[...] = jnp.concatenate([woh[0], woh[1]], axis=1)
    lifted, lift_end = send_maybe(wop, wo.at[z, p, yh % 2], lift)

    def ring_step(step):
        for way, to in ((0, up), (1, down)):
            ring[way, step - 1].wait_recv()
            at = tk.at[(z + 8 - step) % 8 if way == 0 else (z + step) % 8]
            if step == 3:
                at = at.at[pl.ds(128 * way, 128)]
            ring[way, step] = send(at, at, to)

    ring_step(1)
    first.x_forward(0)
    first.y_forward()
    ring_step(2)
    first.x_forward(-1)
    first.x_forward(1)
    first.y_last()
    own_w1.wait()
    first.share(0)
    ring_step(3)
    lifted.wait_recv()
    second.y_own(w2(0, 0, p))
    first.x_forward(2)
    first.share(-1)
    first.share(1)
    second.x_send(0)
    ring[0, 3].wait_recv()
    ring[1, 3].wait_recv()

    def product(dx):
        first.sib[dx].wait_recv()
        total = None
        for k in range(2):
            at = 2 * ((x + dx) % 4) + k
            new = jnp.dot(tk[at], wi[at].reshape(384, 768), preferred_element_type=F32)
            total = new if total is None else total + new
        return total

    acc[...] = product(0)
    second.y_forward()
    acc[...] += product(-1)
    second.x_forward(0)
    acc[...] += product(1)
    first.x_last()
    first.share(2)
    second.y_last()
    second.share(0)
    acc[...] += product(2)

    @pl.loop(0, 16)
    def _(i):
        rows = pl.ds(pl.multiple_of(i * 16, 16), 16)
        hid[rows] = gelu(acc[rows]).astype(BF16)

    second.x_forward(-1)
    second.x_forward(1)
    second.x_forward(2)
    second.share(-1)
    second.share(1)
    second.x_last()
    second.share(2)
    for dx in (0, -1, 1, 2):
        second.sib[dx].wait_recv()

    place = {4: 0, 3: 1, -3: 2, 2: 3, -2: 4, 1: 5, -1: 6, 0: 7}

    def partial(distance):
        weights = wo[(z + 8 + distance) % 8].reshape(768, 384)
        part[place[distance]] = jnp.dot(hid[...], weights, preferred_element_type=F32)

    moved = {}

    def pass_on(name, k, distance):
        for way, to in ((0, up), (1, down)):
            low = (way == 0) == (name == "a")
            rows = slice(0, 128) if low else slice(128, 256)
            value = part[place[distance if way == 0 or distance == 4 else -distance], rows]
            slot = 2 * k if name == "a" else 2 * k + 1
            if k:
                moved[way, name, k - 1].wait_recv()
                value = value + rs_in[way, slot - 2].astype(F32)
            rs_out[way, slot] = value.astype(BF16)
            moved[way, name, k] = send(rs_out.at[way, slot], rs_in.at[way, slot], to)

    partial(4)
    pass_on("a", 0, 4)
    partial(3)
    partial(-3)
    pass_on("b", 0, 3)
    partial(2)
    partial(-2)
    pass_on("a", 1, 3)
    pass_on("b", 1, 2)
    partial(1)
    partial(-1)
    pass_on("a", 2, 2)
    partial(0)
    pass_on("b", 2, 1)
    pass_on("a", 3, 1)
    moved[0, "b", 2].wait_recv()
    moved[1, "b", 2].wait_recv()
    mine = {}
    last = {}
    for half in range(2):
        rows = slice(128 * half, 128 * half + 128)
        moved[half, "a", 3].wait_recv()
        total = part[place[0], rows] + rs_in[half, 6].astype(F32) + rs_in[1 - half, 5].astype(F32)
        low, high = total[:, :192], total[:, 192:]
        end_out[half] = jnp.where(yl == 0, high, low).astype(BF16)
        last[half] = send(end_out.at[half], end_in.at[half], pair)
        part[place[4], rows, :192] = jnp.where(yl == 0, low, high)
    for half in range(2):
        rows = slice(128 * half, 128 * half + 128)
        last[half].wait_recv()
        out_ref[rows] = (part[place[4], rows, :192] + end_in[half].astype(F32)).astype(BF16)

    for made in started:
        made.wait_send()
    halves[0][1]()
    halves[1][1]()
    lift_end()


def local(tokens, w_in, w_out):
    return pl.pallas_call(
        kernel,
        name="mlp_block",
        out_shape=jax.ShapeDtypeStruct((256, 192), BF16),
        in_specs=[pl.BlockSpec(memory_space=pl.ANY)] * 3,
        out_specs=pl.BlockSpec(memory_space=pltpu.VMEM),
        scratch_shapes=[
            pltpu.VMEM((8, 256, 384), BF16),
            pltpu.VMEM((8, 2, 2, 96, 768), BF16),
            pltpu.VMEM((8, 2, 2, 192, 384), BF16),
            pltpu.VMEM((2, 256, 192), BF16),
            pltpu.VMEM((2, 192, 192), BF16),
            pltpu.VMEM((192, 384), BF16),
            pltpu.VMEM((256, 768), BF16),
            pltpu.VMEM((256, 768), F32),
            pltpu.VMEM((8, 256, 384), F32),
            pltpu.VMEM((2, 7, 128, 384), BF16),
            pltpu.VMEM((2, 7, 128, 384), BF16),
            pltpu.VMEM((2, 128, 192), BF16),
            pltpu.VMEM((2, 128, 192), BF16),
            pltpu.SemaphoreType.DMA((SEMS,)),
            pltpu.SemaphoreType.DMA((SEMS + 2,)),
            pltpu.SemaphoreType.DMA((2,)),
        ],
        compiler_params=pltpu.CompilerParams(collective_id=0, has_side_effects=True, vmem_limit_bytes=48 * 2**20),
        cost_estimate=pl.CostEstimate(flops=4 * 256 * 3072 * 768, bytes_accessed=2**20, transcendentals=2**18),
    )(tokens, w_in, w_out)


def solution(mesh):
    placed = (P("row", "col"), P("row", "col"), P("row", "col"))
    return jax.shard_map(local, mesh=mesh, in_specs=placed, out_specs=P("row", "col"), check_vma=False)
```

time: 393 us -> 106 us (0.27)
  waiting for transfers between devices: 366 us -> 0 us
  Pallas kernels: 0 us -> 103 us
  matrix products: 13.5 us -> 0 us
  between operations: 13.1 us -> 0.04 us
    all_gather x4 -> x0, waiting for transfers between devices: 364 us -> none  [the longest x1 145 us: local(): hidden_rows = lax.all_gather(hidden, 'col', axis=1, tiled=True)]
    pallas_call x0 -> x1, Pallas kernels: none -> 103 us  [local(): pl.pallas_call(kernel, name='mlp_block', out_shape=jax.ShapeDtypeStruct((...]
    dot_general x2 -> x0, matrix products: 13.5 us -> none  [the longest x1 7.02 us: local(): jnp.dot(columns, lax.all_gather(w_out, 'row', axis=0, tiled=True), prefer...]
  transfers between devices with their start and end apart: 4 -> 0, of which waited for: 4 -> 0; matrix products, arithmetic and copies ran while one was open for 2% -> 0% of each run, Pallas kernels for 0% -> 0%
where the time goes in v1:
time: 106 us; the launch traced here: 105 us
  Pallas kernels  103 us (97%)
  local copies, waits for them, and re-layouts  2.67 us (3%)
    pallas_call x1, Pallas kernels, local(): pl.pallas_call(kernel, name='mlp_block', out_shape=jax.ShapeDtypeStruct((...  103 us

profile of v1, /device:TPU:1, one launch (start us, length us, event | category | flops | bytes accessed | tf_op | source)
XLA Modules:
  0.0 105.5 jit_solution(5904698008639771028)
XLA Ops:
  0.0 0.0 copy-start.1
  0.0 1.0 copy.4.tok_ref
  1.0 0.0 copy-done.1
  1.0 0.0 copy-start
  1.1 0.1 copy.5.wout_ref
  1.2 0.8 copy-done
  2.0 102.8 %mlp_block.1 = bf16[256,192]{1,0:T(8,128)(2,1)S(1)} custom-call(bf16[256,192]{1,0:T(8,128)(2,1)S(1)} %copy.4.tok_ref, bf16[96,768]{1,0:T(8,128)(2,1)S(1)} %copy-done, bf16[384,192]{1,0:T(8,128)(2,1)S(1)} %copy.5.wout_ref), custom_call_target="tpu_custom_call" | custom-call | flops 2415919104 | bytes 1048576 | tf_op jit(solution)/shard_map/mlp_block/pallas_call | solution.py:308
  104.7 0.7 copy.6
Async XLA Ops:
  0.0 1.0 copy-start.1
  1.0 0.9 copy-start

commit v2 on v1

v2 whole, which is shorter than its diff:
```python
import jax
import jax.numpy as jnp
from jax import lax
from jax.experimental import pallas as pl
from jax.experimental.pallas import tpu as pltpu
from jax.sharding import PartitionSpec as P

MESH = pl.DeviceIdType.MESH
BF16, F32 = jnp.bfloat16, jnp.float32
SEMS = 92


def horner(v, terms):
    total = jnp.full_like(v, terms[0])
    for term in terms[1:]:
        total = total * v + term
    return total


ERF_NEAR = (7.853861353153693e-5, -8.010193625184903e-4, 5.188327685732524e-3, -2.685381193529856e-2,
            1.128358514861418e-1, -3.761262582423300e-1, 1.128379165726710e0)
ERFC_MID = (2.326819970068386e-2, -1.387039388740657e-1, 3.687424674597105e-1, -5.824733027278666e-1,
            6.210004621745983e-1, -4.944515323274145e-1, 3.404879937665872e-1, -2.741127028184656e-1,
            5.638259427386472e-1)
ERFC_FAR = (-1.047766399936249e1, 1.297719955372516e1, -7.495518717768503e0, 2.921019019210786e0,
            -1.015265279202700e0, 4.218463358204948e-1, -2.820767439740514e-1, 5.641895067754075e-1)


def gelu(v):
    u = v * (-(0.5**0.5))
    square = u * u
    size = jnp.maximum(jnp.abs(u), 0.5)
    near = 1.0 - u * horner(jnp.minimum(square, 1.0), ERF_NEAR)
    inverse = 1.0 / size
    y = inverse * inverse
    series = jnp.where(size < 2.0, horner(jnp.minimum(y, 1.0), ERFC_MID), horner(jnp.minimum(y, 0.25), ERFC_FAR))
    tail = jnp.exp(-square) * inverse * series
    far = jnp.where(u < 0.0, 2.0 - tail, tail)
    return 0.5 * v * jnp.where(jnp.abs(u) < 1.0, near, far)


def kernel(tok_ref, win_ref, wout_ref, out_ref, tk, wi, wo, tokp, stage, hid, acc, part, rs_out, rs_in, swap_out, swap_in,
           send_sem, recv_sem, local_sem):
    r, c = lax.axis_index("row"), lax.axis_index("col")
    x, yh, p, z, yl = r // 8, (r // 2) % 4, r % 2, c // 2, c % 2

    def device(x, yh, p, z, yl):
        return ((x % 4) * 8 + (yh % 4) * 2 + p, (z % 8) * 2 + yl)

    right, left = device(x + 1, yh, p, z, yl), device(x + 3, yh, p, z, yl)
    far_y, near_y = device(x, yh + 1, p, z, yl), device(x, yh + 3, p, z, yl)
    up, down = device(x, yh, p, z + 1, yl), device(x, yh, p, z + 7, yl)
    up_pair, down_pair = device(x, yh, p, z + 1, 1 - yl), device(x, yh, p, z + 7, 1 - yl)
    pair, sibling = device(x, yh, p, z, 1 - yl), device(x, yh, 1 - p, z, yl)

    other_x = (z // 2 + 4 - x) % 4
    spread = device(other_x, 2 * ((yh // 2 + z + yl) % 2) + yl, p, z, yh % 2)
    top = (yh // 2 + z + yh) % 2
    spread_from = device(other_x, 2 * top + yl, p, z, yh % 2)
    lift = device(x, yh, p, 2 * other_x + top, yl)
    lift_from = device(x, yh, p, 2 * ((z // 2 + x) % 4) + top, yl)

    sems = [0]
    started = []

    def copy(src, dst, to):
        k = sems[0]
        sems[0] += 1
        return pltpu.make_async_remote_copy(
            src_ref=src, dst_ref=dst, send_sem=send_sem.at[k], recv_sem=recv_sem.at[k], device_id=to, device_id_type=MESH
        )

    def send(src, dst, to):
        made = copy(src, dst, to)
        made.start()
        started.append(made)
        return made

    def sent(made):
        made.wait_send()
        started[:] = [other for other in started if other is not made]

    def send_maybe(src, dst, to):
        k = sems[0]
        made = copy(src, dst, to)
        here = jnp.logical_and(to[0] == r, to[1] == c)

        @pl.when(here)
        def _():
            pltpu.make_async_copy(src, dst, recv_sem.at[k]).start()

        @pl.when(jnp.logical_not(here))
        def _():
            made.start()

        def end():
            @pl.when(jnp.logical_not(here))
            def _():
                made.wait_send()

        return made, end

    def w1(dx, dy, core, half=None):
        px, py = (x + dx) % 4, (yh + dy) % 4
        at = wi.at[2 * px + py // 2, py % 2, core]
        return at if half is None else at.at[pl.ds(48 * half, 48)]

    def w1_group(dx, core):
        return wi.at[pl.ds(2 * ((x + dx) % 4), 2), :, core]

    def w2(dx, dy, core, half=None):
        px, py = (x + dx) % 4, (yh + dy) % 4
        at = wo.at[2 * ((z // 2 + px) % 4) + (z + py // 2 + py) % 2, core, py % 2]
        return at if half is None else at.at[pl.ds(96 * half, 96)]

    def w2_group(dx, core):
        return wo.at[pl.ds(2 * ((z // 2 + x + dx) % 4), 2), core]

    class Gather:
        def __init__(self, at, group, far):
            self.at, self.group, self.by_y = at, group, far
            self.x, self.xh, self.yh, self.fh, self.sib = {}, {}, {}, {}, {}

        def y_own(self, src):
            self.y = {d: send(src, self.at(0, 0, p), to) for d, to in ((-1, far_y), (1, near_y))}

        def y_forward(self):
            self.y[-1].wait_recv()
            self.yh[0] = send(self.at(0, -1, p, 0), self.at(0, -1, p, 0), far_y)
            self.x_send(-1)
            self.y[1].wait_recv()
            self.yh[1] = send(self.at(0, 1, p, 1), self.at(0, 1, p, 1), near_y)
            self.x_send(1)

        def y_last(self):
            self.yh[0].wait_recv()
            self.yh[1].wait_recv()
            self.x_send(2)

        def x_send(self, dy, src=None):
            src = self.at(0, dy, p) if src is None else src
            for d, to in ((-1, right), (1, left)):
                self.x[d, dy] = send(src, self.at(0, dy, p), to)

        def x_forward(self, dy):
            self.x[-1, dy].wait_recv()
            if dy and self.by_y:
                self.x[1, dy].wait_recv()
                return
            self.xh[0, dy] = send(self.at(-1, dy, p, 0), self.at(-1, dy, p, 0), right)
            self.x[1, dy].wait_recv()
            self.xh[1, dy] = send(self.at(1, dy, p, 1), self.at(1, dy, p, 1), left)

        def far_own(self):
            if not self.by_y:
                return
            for made in self.xh.values():
                made.wait_recv()
            self.far = {d: send(self.at(2, 0, p), self.at(2, 0, p), to) for d, to in ((-1, far_y), (1, near_y))}

        def far_forward(self):
            if not self.by_y:
                return
            self.far[-1].wait_recv()
            self.fh[0] = send(self.at(2, -1, p, 0), self.at(2, -1, p, 0), far_y)
            self.far[1].wait_recv()
            self.fh[1] = send(self.at(2, 1, p, 1), self.at(2, 1, p, 1), near_y)

        def far_last(self):
            for made in (self.fh if self.by_y else self.xh).values():
                made.wait_recv()

        def share(self, dx):
            self.sib[dx] = send(self.group(dx, p), self.group(dx, p), sibling)

    first, second = Gather(w1, w1_group, False), Gather(w2, w2_group, False)

    own_w1 = pltpu.make_async_copy(win_ref, w1(0, 0, p), local_sem.at[0])
    own_tok = pltpu.make_async_copy(tok_ref, tokp.at[yl], local_sem.at[1])
    own_w1.start()
    own_tok.start()

    barrier = pltpu.get_barrier_semaphore()
    greeted = [right, left, far_y, near_y, up, down, up_pair, down_pair, pair, sibling, spread_from, lift_from]
    for to in greeted:
        pl.semaphore_signal(barrier, inc=1, device_id=to, device_id_type=MESH)
    pl.semaphore_wait(barrier, len(greeted))

    tok_pair = send(tok_ref, tokp.at[yl], pair)
    first.x_send(0, win_ref)
    sent(tok_pair)
    first.y_own(win_ref)

    tok_pair.wait_recv()
    own_tok.wait()
    tk[z] = tokp[...].reshape(384, 256).T
    ring = {}

    def ring_step(step, halves=(0, 1)):
        for half in halves:
            for way, to in ((0, up), (1, down)):
                if step:
                    if step == 3 and half != way:
                        continue
                    ring[way, half, step - 1].wait_recv()
                at = tk.at[(z + 8 - step) % 8 if way == 0 else (z + step) % 8, pl.ds(128 * half, 128)]
                ring[way, half, step] = send(at, at, to)

    ring_step(0)
    spreading, spread_end = send_maybe(wout_ref, stage, spread)
    first.x_forward(0)
    ring_step(1)
    first.y_forward()
    spreading.wait_recv()
    lifting, lift_end = send_maybe(stage, wo.at[z, p, yh % 2], lift)
    ring_step(2)
    first.y_last()
    first.far_own()
    own_w1.wait()
    first.share(0)
    first.x_forward(-1)
    first.x_forward(1)
    ring_step(3)
    lifting.wait_recv()
    second.y_own(w2(0, 0, p))
    second.x_send(0)
    first.far_forward()
    first.x_forward(2)
    first.share(-1)
    first.share(1)
    ring[0, 0, 3].wait_recv()
    ring[1, 1, 3].wait_recv()
    ring[0, 1, 2].wait_recv()
    ring[1, 0, 2].wait_recv()

    def product(dx):
        first.sib[dx].wait_recv()
        total = None
        for k in range(2):
            at = 2 * ((x + dx) % 4) + k
            new = jnp.dot(tk[at], wi[at].reshape(384, 768), preferred_element_type=F32)
            total = new if total is None else total + new
        return total

    acc[...] = product(0)
    second.x_forward(0)
    acc[...] += product(-1)
    second.y_forward()
    acc[...] += product(1)
    first.far_last()
    first.share(2)
    second.y_last()
    second.far_own()
    second.share(0)
    acc[...] += product(2)

    @pl.loop(0, 16)
    def _(i):
        rows = pl.ds(pl.multiple_of(i * 16, 16), 16)
        hid[rows] = gelu(acc[rows]).astype(BF16)

    second.x_forward(-1)
    second.x_forward(1)
    second.far_forward()
    second.x_forward(2)
    second.share(-1)
    second.share(1)
    second.far_last()
    second.share(2)
    for dx in (0, -1, 1, 2):
        second.sib[dx].wait_recv()

    place = {4: 0, 3: 1, -3: 2, 2: 3, -2: 4, 1: 5, -1: 6, 0: 7}

    def partial(distance):
        at = (z + 8 + distance) % 8
        weights = jnp.concatenate([wo[at, 0].reshape(384, 384), wo[at, 1].reshape(384, 384)], axis=1)
        value = lax.dot_general(weights, hid[...], (((1,), (1,)), ((), ())), preferred_element_type=F32)
        part[place[distance]] = value.reshape(2, 192, 256)

    moved, swapped = {}, {}

    def swap(distance):
        slot = distance % 3
        swap_out[slot] = part[place[distance], 1 - yl].astype(BF16)
        swapped[distance] = send(swap_out.at[slot], swap_in.at[slot], pair)

    def pass_on(name, k, distance):
        for turn in range(2):
            if distance == 1 and turn == 0:
                continue
            feature = yl if turn else 1 - yl
            for way, to, cross in ((0, up, up_pair), (1, down, down_pair)):
                half = way if name == "a" else 1 - way
                lanes = slice(128 * half, 128 * half + 128)
                sign = distance if way == 0 or distance == 4 else -distance
                value = part[place[sign], feature, :, lanes]
                slot = (2 * k if name == "a" else 2 * k + 1) * 2 + turn
                if distance == 1:
                    if name == "b":
                        swapped[sign].wait_recv()
                    value = value + swap_in[sign % 3, :, lanes].astype(F32)
                    moved[way, name, k - 1, 0].wait_recv()
                    value = value + rs_in[way, slot - 5].astype(F32)
                if k:
                    moved[way, name, k - 1, turn].wait_recv()
                    value = value + rs_in[way, slot - 4].astype(F32)
                rs_out[way, slot] = value.astype(BF16)
                to = cross if distance == 2 and turn == 0 else to
                moved[way, name, k, turn] = send(rs_out.at[way, slot], rs_in.at[way, slot], to)

    partial(4)
    pass_on("a", 0, 4)
    partial(3)
    partial(-3)
    pass_on("b", 0, 3)
    partial(1)
    swap(1)
    partial(-1)
    swap(-1)
    partial(2)
    partial(-2)
    pass_on("a", 1, 3)
    pass_on("b", 1, 2)
    partial(0)
    swap(0)
    pass_on("a", 2, 2)
    old = len(started)
    pass_on("b", 2, 1)
    pass_on("a", 3, 1)
    fresh = len(started) - old
    while len(started) > fresh:
        sent(started[0])
    spread_end()
    lift_end()
    swapped[0].wait_recv()
    mine = [part[place[0], yl, :, 128 * half : 128 * half + 128] for half in range(2)]
    mine = [mine[half] + swap_in[0, :, 128 * half : 128 * half + 128].astype(F32) for half in range(2)]
    for half in range(2):
        moved[1 - half, "b", 2, 1].wait_recv()
        mine[half] = mine[half] + rs_in[1 - half, 11].astype(F32)
    for half in range(2):
        moved[half, "a", 3, 1].wait_recv()
        value = mine[half] + rs_in[half, 13].astype(F32)
        out_ref[:, 128 * half : 128 * half + 128] = value.astype(BF16)

    for made in started:
        made.wait_send()


def local(tokens, w_in, w_out):
    out = pl.pallas_call(
        kernel,
        name="mlp_block",
        out_shape=jax.ShapeDtypeStruct((192, 256), BF16),
        in_specs=[pl.BlockSpec(memory_space=pltpu.HBM)] * 3,
        out_specs=pl.BlockSpec(memory_space=pltpu.VMEM),
        scratch_shapes=[
            pltpu.VMEM((8, 256, 384), BF16),
            pltpu.VMEM((8, 2, 2, 96, 768), BF16),
            pltpu.VMEM((8, 2, 2, 192, 384), BF16),
            pltpu.VMEM((2, 192, 256), BF16),
            pltpu.VMEM((192, 384), BF16),
            pltpu.VMEM((256, 768), BF16),
            pltpu.VMEM((256, 768), F32),
            pltpu.VMEM((8, 2, 192, 256), F32),
            pltpu.VMEM((2, 14, 192, 128), BF16),
            pltpu.VMEM((2, 14, 192, 128), BF16),
            pltpu.VMEM((3, 192, 256), BF16),
            pltpu.VMEM((3, 192, 256), BF16),
            pltpu.SemaphoreType.DMA((SEMS,)),
            pltpu.SemaphoreType.DMA((SEMS,)),
            pltpu.SemaphoreType.DMA((2,)),
        ],
        compiler_params=pltpu.CompilerParams(collective_id=0, has_side_effects=True, vmem_limit_bytes=60 * 2**20),
        cost_estimate=pl.CostEstimate(flops=4 * 256 * 3072 * 768, bytes_accessed=2**20, transcendentals=2**18),
    )(tokens.T, w_in, w_out.T)
    return out.T


def solution(mesh):
    placed = (P("row", "col"), P("row", "col"), P("row", "col"))
    return jax.shard_map(local, mesh=mesh, in_specs=placed, out_specs=P("row", "col"), check_vma=False)
```

time: 106 us -> 90.6 us (0.85)
  Pallas kernels: 103 us -> 88.9 us
  local copies, waits for them, and re-layouts: 2.67 us -> 1.54 us
    pallas_call x1, Pallas kernels: 103 us -> 88.9 us  [local(): pl.pallas_call(kernel, name='mlp_block', out_shape=jax.ShapeDtypeStruct((...]
where the time goes in v2:
time: 90.6 us; the launch traced here: 90.4 us
  Pallas kernels  88.9 us (98%)
  local copies, waits for them, and re-layouts  1.54 us (2%)
    pallas_call x1, Pallas kernels, local(): pl.pallas_call(kernel, name='mlp_block', out_shape=jax.ShapeDtypeStruct((...  88.9 us

profile of v2, /device:TPU:1, one launch (start us, length us, event | category | flops | bytes accessed | tf_op | source)
XLA Modules:
  0.0 90.4 jit_solution(111866970401797624)
XLA Ops:
  0.0 88.9 %mlp_block.1 = bf16[192,256]{1,0:T(8,128)(2,1)} custom-call(bf16[192,256]{1,0:T(8,128)(2,1)} %bitcast.5, bf16[96,768]{1,0:T(8,128)(2,1)} %win_ref.1, bf16[192,384]{1,0:T(8,128)(2,1)} %bitcast.4), custom_call_target="tpu_custom_call" | custom-call | flops 2415919104 | bytes 1048576 | tf_op jit(solution)/shard_map/mlp_block/pallas_call | solution.py:352
  88.9 1.5 %copy.5 = bf16[256,192]{0,1:T(8,128)(2,1)} copy(bf16[256,192]{0,1:T(8,128)(2,1)} %bitcast.3) | data formatting | bytes 196608

commit v3 on v2

--- a/solution.py
+++ b/solution.py
@@ -7,7 +7,7 @@
 
 MESH = pl.DeviceIdType.MESH
 BF16, F32 = jnp.bfloat16, jnp.float32
-SEMS = 92
+SEMS = 102
 
 
 def horner(v, terms):
@@ -122,15 +122,24 @@
             self.x, self.xh, self.yh, self.fh, self.sib = {}, {}, {}, {}, {}
 
         def y_own(self, src):
-            self.y = {d: send(src, self.at(0, 0, p), to) for d, to in ((-1, far_y), (1, near_y))}
+            size = src.shape[0] // 2
+            self.y = {}
+            for first_half in range(2):
+                for d, to in ((-1, far_y), (1, near_y)):
+                    half = first_half if d == -1 else 1 - first_half
+                    self.y[d, half] = send(src.at[pl.ds(size * half, size)], self.at(0, 0, p, half), to)
 
         def y_forward(self):
-            self.y[-1].wait_recv()
+            self.y[-1, 0].wait_recv()
             self.yh[0] = send(self.at(0, -1, p, 0), self.at(0, -1, p, 0), far_y)
-            self.x_send(-1)
-            self.y[1].wait_recv()
+            self.x_send_half(-1, 0)
+            self.y[1, 1].wait_recv()
             self.yh[1] = send(self.at(0, 1, p, 1), self.at(0, 1, p, 1), near_y)
-            self.x_send(1)
+            self.x_send_half(1, 1)
+            self.y[-1, 1].wait_recv()
+            self.x_send_half(-1, 1)
+            self.y[1, 0].wait_recv()
+            self.x_send_half(1, 0)
 
         def y_last(self):
             self.yh[0].wait_recv()
@@ -142,38 +151,38 @@
             for d, to in ((-1, right), (1, left)):
                 self.x[d, dy] = send(src, self.at(0, dy, p), to)
 
+        def x_send_half(self, dy, half):
+            for d, to in ((-1, right), (1, left)):
+                self.x[d, dy, half] = send(self.at(0, dy, p, half), self.at(0, dy, p, half), to)
+
         def x_forward(self, dy):
-            self.x[-1, dy].wait_recv()
-            if dy and self.by_y:
-                self.x[1, dy].wait_recv()
-                return
-            self.xh[0, dy] = send(self.at(-1, dy, p, 0), self.at(-1, dy, p, 0), right)
-            self.x[1, dy].wait_recv()
-            self.xh[1, dy] = send(self.at(1, dy, p, 1), self.at(1, dy, p, 1), left)
+            for d, half, to in ((-1, 0, right), (1, 1, left)):
+                (self.x[d, dy, half] if dy in (-1, 1) else self.x[d, dy]).wait_recv()
+                if not (self.by_y and dy in (-1, 1)):
+                    self.xh[half, dy] = send(self.at(d, dy, p, half), self.at(d, dy, p, half), to)
+
+        def x_rest(self):
+            for dy in (-1, 1):
+                self.x[-1, dy, 1].wait_recv()
+                self.x[1, dy, 0].wait_recv()
 
         def far_own(self):
-            if not self.by_y:
-                return
-            for made in self.xh.values():
-                made.wait_recv()
-            self.far = {d: send(self.at(2, 0, p), self.at(2, 0, p), to) for d, to in ((-1, far_y), (1, near_y))}
-
-        def far_forward(self):
-            if not self.by_y:
-                return
-            self.far[-1].wait_recv()
-            self.fh[0] = send(self.at(2, -1, p, 0), self.at(2, -1, p, 0), far_y)
-            self.far[1].wait_recv()
-            self.fh[1] = send(self.at(2, 1, p, 1), self.at(2, 1, p, 1), near_y)
+            self.xh[0, 0].wait_recv()
+            self.xh[1, 0].wait_recv()
+            self.far = [send(self.at(2, 0, p), self.at(2, 0, p), to) for to in (far_y, near_y)]
 
         def far_last(self):
-            for made in (self.fh if self.by_y else self.xh).values():
-                made.wait_recv()
+            for key, made in self.xh.items():
+                if not (self.by_y and key[1] == 0):
+                    made.wait_recv()
+            if self.by_y:
+                for made in self.far:
+                    made.wait_recv()
 
         def share(self, dx):
             self.sib[dx] = send(self.group(dx, p), self.group(dx, p), sibling)
 
-    first, second = Gather(w1, w1_group, False), Gather(w2, w2_group, False)
+    first, second = Gather(w1, w1_group, True), Gather(w2, w2_group, False)
 
     own_w1 = pltpu.make_async_copy(win_ref, w1(0, 0, p), local_sem.at[0])
     own_tok = pltpu.make_async_copy(tok_ref, tokp.at[yl], local_sem.at[1])
@@ -186,15 +195,16 @@
         pl.semaphore_signal(barrier, inc=1, device_id=to, device_id_type=MESH)
     pl.semaphore_wait(barrier, len(greeted))
 
-    tok_pair = send(tok_ref, tokp.at[yl], pair)
-    first.x_send(0, win_ref)
-    sent(tok_pair)
-    first.y_own(win_ref)
-
-    tok_pair.wait_recv()
-    own_tok.wait()
-    tk[z] = tokp[...].reshape(384, 256).T
     ring = {}
+
+    def product(dx):
+        first.sib[dx].wait_recv()
+        total = None
+        for k in range(2):
+            at = 2 * ((x + dx) % 4) + k
+            new = jnp.dot(tk[at], wi[at].reshape(384, 768), preferred_element_type=F32)
+            total = new if total is None else total + new
+        return total
 
     def ring_step(step, halves=(0, 1)):
         for half in halves:
@@ -206,63 +216,64 @@
                 at = tk.at[(z + 8 - step) % 8 if way == 0 else (z + step) % 8, pl.ds(128 * half, 128)]
                 ring[way, half, step] = send(at, at, to)
 
-    ring_step(0)
+    def tokens_begin():
+        tok_pair.wait_recv()
+        own_tok.wait()
+        tk[z] = tokp[...].reshape(384, 256).T
+        ring_step(0)
+
     spreading, spread_end = send_maybe(wout_ref, stage, spread)
+    first.y_own(win_ref)
+    first.x_send(0, win_ref)
     first.x_forward(0)
-    ring_step(1)
-    first.y_forward()
+    tok_pair = send(tok_ref, tokp.at[yl], pair)
     spreading.wait_recv()
     lifting, lift_end = send_maybe(stage, wo.at[z, p, yh % 2], lift)
-    ring_step(2)
+    first.y_forward()
+    tokens_begin()
+    first.far_own()
+    first.x_forward(-1)
+    ring_step(1, (0,))
+    lifting.wait_recv()
+    second.y_own(w2(0, 0, p))
     first.y_last()
-    first.far_own()
+    second.x_send(0)
+    ring_step(1, (1,))
+    first.x_forward(1)
     own_w1.wait()
     first.share(0)
-    first.x_forward(-1)
-    first.x_forward(1)
-    ring_step(3)
-    lifting.wait_recv()
-    second.y_own(w2(0, 0, p))
-    second.x_send(0)
-    first.far_forward()
+    ring_step(2, (0,))
     first.x_forward(2)
+    ring_step(2, (1,))
+    second.x_forward(0)
+    first.x_rest()
     first.share(-1)
     first.share(1)
+    second.y_forward()
+    ring_step(3)
+    first.far_last()
+    first.share(2)
+    second.y_last()
+    second.share(0)
+    second.x_forward(-1)
     ring[0, 0, 3].wait_recv()
     ring[1, 1, 3].wait_recv()
     ring[0, 1, 2].wait_recv()
     ring[1, 0, 2].wait_recv()
 
-    def product(dx):
-        first.sib[dx].wait_recv()
-        total = None
-        for k in range(2):
-            at = 2 * ((x + dx) % 4) + k
-            new = jnp.dot(tk[at], wi[at].reshape(384, 768), preferred_element_type=F32)
-            total = new if total is None else total + new
-        return total
-
     acc[...] = product(0)
-    second.x_forward(0)
     acc[...] += product(-1)
-    second.y_forward()
+    second.x_forward(1)
     acc[...] += product(1)
-    first.far_last()
-    first.share(2)
-    second.y_last()
-    second.far_own()
-    second.share(0)
     acc[...] += product(2)
+    second.x_forward(2)
 
     @pl.loop(0, 16)
     def _(i):
         rows = pl.ds(pl.multiple_of(i * 16, 16), 16)
         hid[rows] = gelu(acc[rows]).astype(BF16)
 
-    second.x_forward(-1)
-    second.x_forward(1)
-    second.far_forward()
-    second.x_forward(2)
+    second.x_rest()
     second.share(-1)
     second.share(1)
     second.far_last()
@@ -352,7 +363,7 @@
     out = pl.pallas_call(
         kernel,
         name="mlp_block",
-        out_shape=jax.ShapeDtypeStruct((192, 256), BF16),
+        out_shape=pltpu.VMEM((192, 256), BF16),
         in_specs=[pl.BlockSpec(memory_space=pltpu.HBM)] * 3,
         out_specs=pl.BlockSpec(memory_space=pltpu.VMEM),
         scratch_shapes=[

time: 90.6 us -> 84.1 us (0.928)
  Pallas kernels: 88.9 us -> 82.9 us
    pallas_call x1, Pallas kernels: 88.9 us -> 82.9 us  [local(): pl.pallas_call(kernel, name='mlp_block', out_shape=pltpu.VMEM((192, 256),...]
where the time goes in v3:
time: 84.1 us; the launch traced here: 83.5 us
  Pallas kernels  82.9 us (99%)
    pallas_call x1, Pallas kernels, local(): pl.pallas_call(kernel, name='mlp_block', out_shape=pltpu.VMEM((192, 256),...  82.9 us

profile of v3, /device:TPU:1, one launch (start us, length us, event | category | flops | bytes accessed | tf_op | source)
XLA Modules:
  0.0 83.5 jit_solution(3101074004401212358)
XLA Ops:
  0.0 82.9 %mlp_block.1 = bf16[192,256]{1,0:T(8,128)(2,1)S(1)} custom-call(bf16[192,256]{1,0:T(8,128)(2,1)} %bitcast.5, bf16[96,768]{1,0:T(8,128)(2,1)} %win_ref.1, bf16[192,384]{1,0:T(8,128)(2,1)} %bitcast.4), custom_call_target="tpu_custom_call" | custom-call | flops 2415919104 | bytes 1048576 | tf_op jit(solution)/shard_map/mlp_block/pallas_call | solution.py:363
  82.9 0.6 copy.5

commit v4 on v3

--- a/solution.py
+++ b/solution.py
@@ -7,7 +7,9 @@
 
 MESH = pl.DeviceIdType.MESH
 BF16, F32 = jnp.bfloat16, jnp.float32
-SEMS = 102
+SEMS = 111
+OUT_SEMS = 30
+SHARED = ("first", "second", "ring", "swap", "sums")
 
 
 def horner(v, terms):
@@ -63,18 +65,30 @@
     sems = [0]
     started = []
 
-    def copy(src, dst, to):
+    out_sems = [len(SHARED)]
+
+    def copy(src, dst, to, shared=None):
         k = sems[0]
         sems[0] += 1
+        if shared is None:
+            j = out_sems[0]
+            out_sems[0] += 1
+        else:
+            j = SHARED.index(shared)
         return pltpu.make_async_remote_copy(
-            src_ref=src, dst_ref=dst, send_sem=send_sem.at[k], recv_sem=recv_sem.at[k], device_id=to, device_id_type=MESH
+            src_ref=src, dst_ref=dst, send_sem=send_sem.at[j], recv_sem=recv_sem.at[k], device_id=to, device_id_type=MESH
         )
 
-    def send(src, dst, to):
-        made = copy(src, dst, to)
+    def send(src, dst, to, shared=None):
+        made = copy(src, dst, to, shared)
         made.start()
-        started.append(made)
+        if shared is None:
+            started.append(made)
         return made
+
+    def sent_all(shared, at):
+        j = SHARED.index(shared)
+        pltpu.make_async_copy(at, at, send_sem.at[j]).wait()
 
     def sent(made):
         made.wait_send()
@@ -119,15 +133,16 @@
     class Gather:
         def __init__(self, at, group, far):
             self.at, self.group, self.by_y = at, group, far
-            self.x, self.xh, self.yh, self.fh, self.sib = {}, {}, {}, {}, {}
-
-        def y_own(self, src):
+            self.name = "first" if far else "second"
+            self.x, self.xh, self.y, self.yh, self.sib = {}, {}, {}, {}, {}
+
+        def y_own(self, src, order=(0, 1)):
             size = src.shape[0] // 2
-            self.y = {}
-            for first_half in range(2):
+            for first_half in order:
                 for d, to in ((-1, far_y), (1, near_y)):
                     half = first_half if d == -1 else 1 - first_half
-                    self.y[d, half] = send(src.at[pl.ds(size * half, size)], self.at(0, 0, p, half), to)
+                    name = "first" if self.by_y else None
+                    self.y[d, half] = send(src.at[pl.ds(size * half, size)], self.at(0, 0, p, half), to, name)
 
         def y_forward(self):
             self.y[-1, 0].wait_recv()
@@ -142,34 +157,34 @@
             self.x_send_half(1, 0)
 
         def y_last(self):
-            self.yh[0].wait_recv()
-            self.yh[1].wait_recv()
-            self.x_send(2)
+            for half in range(2):
+                self.yh[half].wait_recv()
+                self.x_send_half(2, half)
 
         def x_send(self, dy, src=None):
             src = self.at(0, dy, p) if src is None else src
             for d, to in ((-1, right), (1, left)):
-                self.x[d, dy] = send(src, self.at(0, dy, p), to)
+                self.x[d, dy] = send(src, self.at(0, dy, p), to, self.name)
 
         def x_send_half(self, dy, half):
             for d, to in ((-1, right), (1, left)):
-                self.x[d, dy, half] = send(self.at(0, dy, p, half), self.at(0, dy, p, half), to)
+                self.x[d, dy, half] = send(self.at(0, dy, p, half), self.at(0, dy, p, half), to, self.name)
 
         def x_forward(self, dy):
             for d, half, to in ((-1, 0, right), (1, 1, left)):
-                (self.x[d, dy, half] if dy in (-1, 1) else self.x[d, dy]).wait_recv()
+                (self.x[d, dy, half] if dy else self.x[d, dy]).wait_recv()
                 if not (self.by_y and dy in (-1, 1)):
                     self.xh[half, dy] = send(self.at(d, dy, p, half), self.at(d, dy, p, half), to)
 
         def x_rest(self):
-            for dy in (-1, 1):
+            for dy in (-1, 1, 2):
                 self.x[-1, dy, 1].wait_recv()
                 self.x[1, dy, 0].wait_recv()
 
         def far_own(self):
             self.xh[0, 0].wait_recv()
             self.xh[1, 0].wait_recv()
-            self.far = [send(self.at(2, 0, p), self.at(2, 0, p), to) for to in (far_y, near_y)]
+            self.far = [send(self.at(2, 0, p), self.at(2, 0, p), to, self.name) for to in (far_y, near_y)]
 
         def far_last(self):
             for key, made in self.xh.items():
@@ -179,20 +194,26 @@
                 for made in self.far:
                     made.wait_recv()
 
+        def share_far(self, *steps):
+            for dy in steps:
+                self.xh[0, dy].wait_recv()
+                self.xh[1, dy].wait_recv()
+                at = self.at(2, dy, p)
+                self.sib[2, dy] = send(at, at, sibling, self.name)
+
         def share(self, dx):
-            self.sib[dx] = send(self.group(dx, p), self.group(dx, p), sibling)
+            self.sib[dx] = send(self.group(dx, p), self.group(dx, p), sibling, self.name)
 
     first, second = Gather(w1, w1_group, True), Gather(w2, w2_group, False)
 
+    barrier = pltpu.get_barrier_semaphore()
+    greeted = [lift_from, spread_from, far_y, near_y, right, left, up, down, pair, sibling, up_pair, down_pair]
+    for to in greeted:
+        pl.semaphore_signal(barrier, inc=1, device_id=to, device_id_type=MESH)
     own_w1 = pltpu.make_async_copy(win_ref, w1(0, 0, p), local_sem.at[0])
     own_tok = pltpu.make_async_copy(tok_ref, tokp.at[yl], local_sem.at[1])
     own_w1.start()
     own_tok.start()
-
-    barrier = pltpu.get_barrier_semaphore()
-    greeted = [right, left, far_y, near_y, up, down, up_pair, down_pair, pair, sibling, spread_from, lift_from]
-    for to in greeted:
-        pl.semaphore_signal(barrier, inc=1, device_id=to, device_id_type=MESH)
     pl.semaphore_wait(barrier, len(greeted))
 
     ring = {}
@@ -214,7 +235,7 @@
                         continue
                     ring[way, half, step - 1].wait_recv()
                 at = tk.at[(z + 8 - step) % 8 if way == 0 else (z + step) % 8, pl.ds(128 * half, 128)]
-                ring[way, half, step] = send(at, at, to)
+                ring[way, half, step] = send(at, at, to, "ring")
 
     def tokens_begin():
         tok_pair.wait_recv()
@@ -222,39 +243,43 @@
         tk[z] = tokp[...].reshape(384, 256).T
         ring_step(0)
 
-    spreading, spread_end = send_maybe(wout_ref, stage, spread)
+    halves = [pl.ds(96 * half, 96) for half in range(2)]
+    spreading = [send_maybe(wout_ref.at[rows], stage.at[rows], spread) for rows in halves]
     first.y_own(win_ref)
     first.x_send(0, win_ref)
+    tok_pair = send(tok_ref, tokp.at[yl], pair)
     first.x_forward(0)
-    tok_pair = send(tok_ref, tokp.at[yl], pair)
-    spreading.wait_recv()
-    lifting, lift_end = send_maybe(stage, wo.at[z, p, yh % 2], lift)
+    lifting = []
+    for rows, (made, _) in zip(halves, spreading):
+        made.wait_recv()
+        lifting.append(send_maybe(stage.at[rows], wo.at[z, p, yh % 2, rows], lift))
     first.y_forward()
     tokens_begin()
-    first.far_own()
     first.x_forward(-1)
-    ring_step(1, (0,))
-    lifting.wait_recv()
+    for made, _ in lifting:
+        made.wait_recv()
     second.y_own(w2(0, 0, p))
     first.y_last()
     second.x_send(0)
+    ring_step(1, (0,))
+    first.far_own()
     ring_step(1, (1,))
     first.x_forward(1)
     own_w1.wait()
     first.share(0)
+    first.x_forward(2)
     ring_step(2, (0,))
-    first.x_forward(2)
+    second.y_forward()
     ring_step(2, (1,))
     second.x_forward(0)
     first.x_rest()
     first.share(-1)
     first.share(1)
-    second.y_forward()
     ring_step(3)
+    second.y_last()
+    second.share(0)
     first.far_last()
     first.share(2)
-    second.y_last()
-    second.share(0)
     second.x_forward(-1)
     ring[0, 0, 3].wait_recv()
     ring[1, 1, 3].wait_recv()
@@ -262,8 +287,8 @@
     ring[1, 0, 2].wait_recv()
 
     acc[...] = product(0)
+    second.x_forward(1)
     acc[...] += product(-1)
-    second.x_forward(1)
     acc[...] += product(1)
     acc[...] += product(2)
     second.x_forward(2)
@@ -276,10 +301,9 @@
     second.x_rest()
     second.share(-1)
     second.share(1)
-    second.far_last()
-    second.share(2)
-    for dx in (0, -1, 1, 2):
-        second.sib[dx].wait_recv()
+    second.share_far(0, -1, 1, 2)
+    for key in (0, -1, 1, (2, 0), (2, -1), (2, 1), (2, 2)):
+        second.sib[key].wait_recv()
 
     place = {4: 0, 3: 1, -3: 2, 2: 3, -2: 4, 1: 5, -1: 6, 0: 7}
 
@@ -294,7 +318,7 @@
     def swap(distance):
         slot = distance % 3
         swap_out[slot] = part[place[distance], 1 - yl].astype(BF16)
-        swapped[distance] = send(swap_out.at[slot], swap_in.at[slot], pair)
+        swapped[distance] = send(swap_out.at[slot], swap_in.at[slot], pair, "swap")
 
     def pass_on(name, k, distance):
         for turn in range(2):
@@ -318,7 +342,7 @@
                     value = value + rs_in[way, slot - 4].astype(F32)
                 rs_out[way, slot] = value.astype(BF16)
                 to = cross if distance == 2 and turn == 0 else to
-                moved[way, name, k, turn] = send(rs_out.at[way, slot], rs_in.at[way, slot], to)
+                moved[way, name, k, turn] = send(rs_out.at[way, slot], rs_in.at[way, slot], to, "sums")
 
     partial(4)
     pass_on("a", 0, 4)
@@ -336,14 +360,16 @@
     partial(0)
     swap(0)
     pass_on("a", 2, 2)
-    old = len(started)
     pass_on("b", 2, 1)
     pass_on("a", 3, 1)
-    fresh = len(started) - old
-    while len(started) > fresh:
+    while started:
         sent(started[0])
-    spread_end()
-    lift_end()
+    for _, end in spreading + lifting:
+        end()
+    sent_all("first", wi.at[pl.ds(0, 7)])
+    sent_all("second", wo.at[pl.ds(0, 6)])
+    sent_all("ring", tk.at[pl.ds(0, 7)])
+    sent_all("swap", swap_out)
     swapped[0].wait_recv()
     mine = [part[place[0], yl, :, 128 * half : 128 * half + 128] for half in range(2)]
     mine = [mine[half] + swap_in[0, :, 128 * half : 128 * half + 128].astype(F32) for half in range(2)]
@@ -355,8 +381,7 @@
         value = mine[half] + rs_in[half, 13].astype(F32)
         out_ref[:, 128 * half : 128 * half + 128] = value.astype(BF16)
 
-    for made in started:
-        made.wait_send()
+    sent_all("sums", rs_out.at[:, pl.ds(0, 12)])
 
 
 def local(tokens, w_in, w_out):
@@ -379,7 +404,7 @@
             pltpu.VMEM((2, 14, 192, 128), BF16),
             pltpu.VMEM((3, 192, 256), BF16),
             pltpu.VMEM((3, 192, 256), BF16),
-            pltpu.SemaphoreType.DMA((SEMS,)),
+            pltpu.SemaphoreType.DMA((OUT_SEMS,)),
             pltpu.SemaphoreType.DMA((SEMS,)),
             pltpu.SemaphoreType.DMA((2,)),
         ],

time: 84.1 us -> 81.8 us (0.973)
  Pallas kernels: 82.9 us -> 81 us
    pallas_call x1, Pallas kernels: 82.9 us -> 81 us  [local(): pl.pallas_call(kernel, name='mlp_block', out_shape=pltpu.VMEM((192, 256),...]
where the time goes in v4:
time: 81.8 us; the launch traced here: 81.7 us
  Pallas kernels  81 us (99%)
    pallas_call x1, Pallas kernels, local(): pl.pallas_call(kernel, name='mlp_block', out_shape=pltpu.VMEM((192, 256),...  81 us

profile of v4, /device:TPU:1, one launch (start us, length us, event | category | flops | bytes accessed | tf_op | source)
XLA Modules:
  0.0 81.7 jit_solution(17520030137909439806)
XLA Ops:
  0.0 81.0 %mlp_block.1 = bf16[192,256]{1,0:T(8,128)(2,1)S(1)} custom-call(bf16[192,256]{1,0:T(8,128)(2,1)} %bitcast.5, bf16[96,768]{1,0:T(8,128)(2,1)} %win_ref.1, bf16[192,384]{1,0:T(8,128)(2,1)} %bitcast.4), custom_call_target="tpu_custom_call" | custom-call | flops 2415919104 | bytes 1048576 | tf_op jit(solution)/shard_map/mlp_block/pallas_call | solution.py:388
  81.0 0.6 copy.5

commit v5 on v4

--- a/solution.py
+++ b/solution.py
@@ -292,15 +292,15 @@
     acc[...] += product(1)
     acc[...] += product(2)
     second.x_forward(2)
+    second.x_rest()
+    second.share(-1)
+    second.share(1)
 
     @pl.loop(0, 16)
     def _(i):
         rows = pl.ds(pl.multiple_of(i * 16, 16), 16)
         hid[rows] = gelu(acc[rows]).astype(BF16)
 
-    second.x_rest()
-    second.share(-1)
-    second.share(1)
     second.share_far(0, -1, 1, 2)
     for key in (0, -1, 1, (2, 0), (2, -1), (2, 1), (2, 2)):
         second.sib[key].wait_recv()

time: 81.8 us -> 81.5 us (level)
  no operation moved by 1% of the time
where the time goes in v5:
time: 81.5 us; the launch traced here: 81.4 us
  Pallas kernels  80.8 us (99%)
    pallas_call x1, Pallas kernels, local(): pl.pallas_call(kernel, name='mlp_block', out_shape=pltpu.VMEM((192, 256),...  80.8 us

profile of v5, /device:TPU:1, one launch (start us, length us, event | category | flops | bytes accessed | tf_op | source)
XLA Modules:
  0.0 81.4 jit_solution(3004150336794322103)
XLA Ops:
  0.0 80.8 %mlp_block.1 = bf16[192,256]{1,0:T(8,128)(2,1)S(1)} custom-call(bf16[192,256]{1,0:T(8,128)(2,1)} %bitcast.5, bf16[96,768]{1,0:T(8,128)(2,1)} %win_ref.1, bf16[192,384]{1,0:T(8,128)(2,1)} %bitcast.4), custom_call_target="tpu_custom_call" | custom-call | flops 2415919104 | bytes 1048576 | tf_op jit(solution)/shard_map/mlp_block/pallas_call | solution.py:388
  80.8 0.6 copy.5

commit v6 on v5

--- a/solution.py
+++ b/solution.py
@@ -295,13 +295,14 @@
     second.x_rest()
     second.share(-1)
     second.share(1)
+    second.share_far(0, -1)
 
     @pl.loop(0, 16)
     def _(i):
         rows = pl.ds(pl.multiple_of(i * 16, 16), 16)
         hid[rows] = gelu(acc[rows]).astype(BF16)
 
-    second.share_far(0, -1, 1, 2)
+    second.share_far(1, 2)
     for key in (0, -1, 1, (2, 0), (2, -1), (2, 1), (2, 2)):
         second.sib[key].wait_recv()
 

time: 81.5 us -> 81.5 us (level)
  no operation moved by 1% of the time
where the time goes in v6:
time: 81.5 us; the launch traced here: 81.4 us
  Pallas kernels  80.8 us (99%)
    pallas_call x1, Pallas kernels, local(): pl.pallas_call(kernel, name='mlp_block', out_shape=pltpu.VMEM((192, 256),...  80.8 us

profile of v6, /device:TPU:1, one launch (start us, length us, event | category | flops | bytes accessed | tf_op | source)
XLA Modules:
  0.0 81.4 jit_solution(14159002980622367545)
XLA Ops:
  0.0 80.8 %mlp_block.1 = bf16[192,256]{1,0:T(8,128)(2,1)S(1)} custom-call(bf16[192,256]{1,0:T(8,128)(2,1)} %bitcast.5, bf16[96,768]{1,0:T(8,128)(2,1)} %win_ref.1, bf16[192,384]{1,0:T(8,128)(2,1)} %bitcast.4), custom_call_target="tpu_custom_call" | custom-call | flops 2415919104 | bytes 1048576 | tf_op jit(solution)/shard_map/mlp_block/pallas_call | solution.py:389
  80.8 0.6 copy.5
